TPU v7x, 32 devices: a whole 2x2x4 slice. The times are simulated.
32 devices in a mesh: groups: 2 (over x), rows: 16 (over z, y, core).
Axes of the slice: x: 2, y: 2, z: 4, core: 2. Of those that a mesh axis runs over, the one named last changes fastest.
Arguments:
- potential: float32 [256, 256], P(('groups', 'rows')), parts along dimension 0, may hold values from -4 to 6
- near_tiles: bfloat16 [512, 256, 256], P(('groups', 'rows')), parts along dimension 0, may hold values from -1 to 1.25
- far_left: bfloat16 [1536, 64, 256], P(('groups', 'rows')), parts along dimension 0, may hold values from -1 to 1.25
- far_right: bfloat16 [1536, 64, 256], P(('groups', 'rows')), parts along dimension 0, may hold values from -1 to 1.25
- col_owner: int32 [2048, 1], P(('groups', 'rows')), parts along dimension 0, may hold values from 0 to 15; in each aligned block of 64 rows (0 to 63, 64 to 127, ...) at most 8 rows name the same one
- col_local: int32 [2048], P(('groups', 'rows')), parts along dimension 0, may hold values from 0 to 7
- row_owner: int32 [2048, 1], P(('groups', 'rows')), parts along dimension 0, may hold values from 0 to 15; in each aligned block of 64 rows (0 to 63, 64 to 127, ...) at most 8 rows name the same one
- row_local: int32 [2048], P(('groups', 'rows')), parts along dimension 0, may hold values from 0 to 7
- far_rank: int32 [1536], P(('groups', 'rows')), parts along dimension 0, may hold values from 8 to 64
Outputs:
- krylov: float32 [2, 256, 256], P(None, ('groups', 'rows')), parts along dimension 1
- hessen: float32 [2, 6], P('groups'), parts along dimension 0
There are 2 independent parts, one for each index of `groups`. A program takes and returns all parts, laid end to end along the dimension named above; each array names one. Nothing has to cross between parts.
Inputs may be any that keep to these rules, and one draw needn't show every extreme that they name: `col_owner`: among the blocks of one index of rows at most 8 name the same column owner, a bound that some block reaches. `row_owner`: among the blocks of one index of rows at most 8 name the same row owner, a bound that some block reaches.
All inputs are finite; a program needn't handle non-finite values.
Results may differ from a plain program's by a relative error of at most 0.0023.
Values may be sent and summed in bfloat16 or wider, within the bound.
A program may use at most 64 MiB of HBM per device.

v0:
```python
import jax
import jax.numpy as jnp
from jax import lax
from jax.sharding import PartitionSpec as P

EPSILON = 1e-06


def one_hot(index_list, width):
    return (index_list[None, :] == jnp.arange(width, dtype=jnp.int32)[:, None]).astype(jnp.float32)


def on_device(
    potential, near_tiles, far_left, far_right, col_owner, col_local, row_owner, row_local, far_rank
):
    devices = lax.axis_size("rows")
    clusters, leaf_size = potential.shape
    near_count = near_tiles.shape[0]
    panel_count = clusters * devices * leaf_size
    col_dest = col_owner[:, 0]
    row_dest = row_owner[:, 0]
    levels = jnp.arange(far_left.shape[1], dtype=jnp.int32)
    rank_mask = levels[None, :] < far_rank[:, None]
    col_global = col_dest * clusters + col_local
    dense_rows = one_hot(row_dest * clusters + row_local, devices * clusters)

    def product(vector):
        rounded = vector.astype(jnp.bfloat16)
        whole = lax.all_gather(rounded, "rows", axis=0, tiled=True)
        picked = whole[col_global]
        near_out = jnp.einsum(
            "kij,kj->ki", near_tiles, picked[:near_count], preferred_element_type=jnp.float32
        )
        weights = jnp.einsum(
            "krj,kj->kr", far_right, picked[near_count:], preferred_element_type=jnp.float32
        )
        weights = jnp.where(rank_mask, weights, 0.0).astype(jnp.bfloat16)
        far_out = jnp.einsum("krj,kr->kj", far_left, weights, preferred_element_type=jnp.float32)
        block_out = jnp.concatenate([near_out, far_out], axis=0)
        field = jnp.dot(dense_rows, block_out, precision=lax.Precision.HIGHEST)
        result = lax.psum_scatter(field, "rows", scatter_dimension=0, tiled=True)
        return result

    def orthonormal(image, basis_list):
        terms = [jnp.sum(image * column) for column in basis_list]
        sums = lax.psum(jnp.stack(terms), "rows") / panel_count
        remainder = image
        for position, column in enumerate(basis_list):
            remainder = remainder - sums[position] * column
        squared = lax.psum(jnp.sum(remainder * remainder), "rows") / panel_count
        height = jnp.sqrt(squared + EPSILON)
        return (remainder / height, sums, height)

    start_sum = lax.psum(jnp.sum(potential * potential), "rows") / panel_count
    beta = jnp.sqrt(start_sum + EPSILON)
    first_basis = potential / beta
    second_basis, coefs_one, height_one = orthonormal(product(first_basis), [first_basis])
    third_basis, coefs_two, height_two = orthonormal(
        product(second_basis), [first_basis, second_basis]
    )
    krylov = jnp.stack([second_basis, third_basis])
    hessen = jnp.stack([beta, coefs_one[0], height_one, coefs_two[0], coefs_two[1], height_two])[
        None, :
    ]
    return (krylov, hessen)


def solution(mesh):
    placed = (
        P(("groups", "rows"), None),
        P(("groups", "rows"), None, None),
        P(("groups", "rows"), None, None),
        P(("groups", "rows"), None, None),
        P(("groups", "rows"), None),
        P(("groups", "rows")),
        P(("groups", "rows"), None),
        P(("groups", "rows")),
        P(("groups", "rows")),
    )
    return jax.shard_map(
        on_device,
        mesh=mesh,
        in_specs=placed,
        out_specs=(P(None, ("groups", "rows"), None), P("groups", None)),
        check_vma=False,
    )
```

profile of v0, /device:TPU:0, one launch (start us, length us, event | category | flops | bytes accessed | tf_op | source)
XLA Modules:
  0.0 336.5 jit_solution(2684232134041248335)
XLA Ops:
  7.2 1.4 multiply_reduce_fusion.5
  8.7 35.5 %psum.35 = f32[]{:T(128)} all-reduce(f32[]{:T(128)} %multiply_reduce_fusion.5), channel_id=1, replica_groups=mesh['groups'=2,'rows'=16] {'rows'}, use_global_device_ids=true, to_apply=%region_1.0 | all-reduce | flops 1 | bytes 8 | tf_op jit(solution)/shard_map/psum | solution.py:54
  44.9 0.7 compare_select_fusion
  45.6 0.7 fusion.26
  46.3 17.3 %all_gather.6 = bf16[128,256]{1,0:T(8,128)(2,1)S(1)} all-gather(bf16[8,256]{1,0:T(8,128)(2,1)S(1)} %fusion.26), channel_id=1, replica_groups=mesh['groups'=2,'rows'=16] {'rows'}, dimensions={0}, use_global_device_ids=true | all-gather | bytes 69632 | tf_op jit(solution)/shard_map/all_gather | solution.py:29
  63.6 0.7 gather_fusion
  65.0 0.7 copy-done.5
  66.6 0.8 fusion
  67.6 53.9 %reduce-scatter.3.cloned.1.call-done = f32[8,256]{1,0:T(8,128)} async-done(((f32[128,256]{1,0:T(8,128)}), f32[8,256]{1,0:T(8,128)}) %reduce-scatter.3.cloned.1.call-update) | async-done | bytes 8208 | tf_op jit(solution)/shard_map/reduce_scatter | solution.py:41
  121.4 1.3 multiply_reduce_fusion.4
  122.7 30.1 %psum.36 = f32[1]{0:T(128)} all-reduce(f32[1]{0:T(128)} %bitcast.9), channel_id=1, replica_groups=mesh['groups'=2,'rows'=16] {'rows'}, use_global_device_ids=true, to_apply=%region_4.5 | all-reduce | flops 1 | bytes 8 | tf_op jit(solution)/shard_map/psum | solution.py:46
  153.5 1.3 multiply_reduce_fusion.3
  154.8 30.1 %psum.37 = f32[]{:T(128)} all-reduce(f32[]{:T(128)} %multiply_reduce_fusion.3), channel_id=1, replica_groups=mesh['groups'=2,'rows'=16] {'rows'}, use_global_device_ids=true, to_apply=%region_6.7 | all-reduce | flops 1 | bytes 8 | tf_op jit(solution)/shard_map/psum | solution.py:50
  185.6 0.7 fusion.27
  186.3 17.3 %all_gather.7 = bf16[128,256]{1,0:T(8,128)(2,1)S(1)} all-gather(bf16[8,256]{1,0:T(8,128)(2,1)S(1)} %get-tuple-element.6), channel_id=1, replica_groups=mesh['groups'=2,'rows'=16] {'rows'}, dimensions={0}, use_global_device_ids=true | all-gather | bytes 69632 | tf_op jit(solution)/shard_map/all_gather | solution.py:29
  203.6 0.7 gather_fusion.1
  204.3 2.0 fusion.8
  207.4 0.8 fusion.4
  208.3 53.9 %reduce-scatter.5.cloned.1.call-done = f32[8,256]{1,0:T(8,128)} async-done(((f32[128,256]{1,0:T(8,128)}), f32[8,256]{1,0:T(8,128)}) %reduce-scatter.5.cloned.1.call-update) | async-done | bytes 8208 | tf_op jit(solution)/shard_map/reduce_scatter | solution.py:41
  262.2 1.3 multiply_reduce_fusion.2
  263.5 1.4 pad_maximum_fusion.1
  264.9 29.5 %psum.38 = f32[2]{0:T(128)S(1)} all-reduce(f32[2]{0:T(128)S(1)} %pad_maximum_fusion.1), channel_id=1, replica_groups=mesh['groups'=2,'rows'=16] {'rows'}, use_global_device_ids=true, to_apply=%region_10.11 | all-reduce | flops 2 | bytes 16 | tf_op jit(solution)/shard_map/psum | solution.py:46
  294.9 2.7 multiply_reduce_fusion
  297.6 30.1 %psum.39 = f32[]{:T(128)} all-reduce(f32[]{:T(128)} %get-tuple-element.4), channel_id=1, replica_groups=mesh['groups'=2,'rows'=16] {'rows'}, use_global_device_ids=true, to_apply=%region_12.13 | all-reduce | flops 1 | bytes 8 | tf_op jit(solution)/shard_map/psum | solution.py:50
  (41 shorter events, 4.6 us)
Async XLA Ops:
  7.2 57.1 %copy-start = (bf16[16,256,256]{2,1,0:T(8,128)(2,1)S(1)}, bf16[16,256,256]{2,1,0:T(8,128)(2,1)}, u32[]{:S(2)}) copy-start(bf16[16,256,256]{2,1,0:T(8,128)(2,1)} %param.10) | copy-start | bytes 6291460
  7.2 114.2 %reduce-scatter.3.cloned.1.call-start = ((), (), s32[]{:S(2)}) async-start(), calls=%async_computation.2 | async-start | bytes 139264 | tf_op jit(solution)/shard_map/reduce_scatter | solution.py:41
  64.3 1.4 copy-start.5
  64.3 1.9 copy-start.4
  64.3 1.9 copy-start.1
  65.7 0.9 copy-start.6
  65.7 0.9 copy-start.7
  65.7 55.7 %copy-start.3 = (f32[8,256]{1,0:T(8,128)S(1)}, f32[8,256]{1,0:T(8,128)}, u32[]{:S(2)}) copy-start(f32[8,256]{1,0:T(8,128)} %param.9) | copy-start | bytes 24580
  67.5 194.7 %reduce-scatter.5.cloned.1.call-start = ((), (), s32[]{:S(2)}) async-start(), calls=%async_computation.3 | async-start | bytes 139264 | tf_op jit(solution)/shard_map/reduce_scatter | solution.py:41
  204.3 2.8 copy-start.2
Sparse Core Ops, SparseCore 0:
  67.6 53.7 reduce-scatter.2
  208.4 53.7 reduce-scatter.4
where the time goes:
time: 337 us; the launch traced here: 336 us
  blocking collectives  190 us (56%)
  waiting for transfers between devices  108 us (32%)
  between operations  16.9 us (5%)
  other arithmetic  12.3 us (4%)
  matrix products  6.16 us (2%)
    reduce_scatter x2, waiting for transfers between devices, product(): result = lax.psum_scatter(field, 'rows', scatter_dimension=0, tiled=True)  108 us
    psum x2, blocking collectives, orthonormal(): squared = lax.psum(jnp.sum(remainder * remainder), 'rows') / panel_count  60.2 us
    psum x2, blocking collectives, orthonormal(): sums = lax.psum(jnp.stack(terms), 'rows') / panel_count  59.6 us
    psum x1, blocking collectives, on_device(): start_sum = lax.psum(jnp.sum(potential * potential), 'rows') / panel_count  35.5 us
    all_gather x2, blocking collectives, product(): whole = lax.all_gather(rounded, 'rows', axis=0, tiled=True)  34.6 us
  transfers between devices with their start and end apart: 2, of which 2 were waited for; matrix products, arithmetic and copies ran while one was open for 0% of the time, Pallas kernels for 0%

commit v1 on v0

v1 whole, which is shorter than its diff:
```python
import functools

import jax
import jax.numpy as jnp
from jax import lax
from jax.experimental import pallas as pl
from jax.experimental.pallas import tpu as pltpu
from jax.sharding import PartitionSpec as P

EPSILON = 1e-06
MESH = pl.DeviceIdType.MESH


def total(values):
    return jnp.sum(jnp.sum(values, axis=0, keepdims=True), axis=1, keepdims=True)


def kernel(
    n, potential, near_hbm, left_hbm, right_hbm, col_owner, col_local, row_owner, row_local, far_rank,
    krylov, hessen,
    near, left, right, masks, rank_masks, field_one, field_two, whole_p, whole_i, parts_one, parts_two,
    mine, sums, load_sem, send_sem, recv_sem,
):
    me = lax.axis_index("rows")
    clusters, leaf = potential.shape
    blocks = col_owner.shape[0]
    near_count, far_count, rank = near.shape[0], left.shape[0], left.shape[1]
    rows = n * clusters
    panels = rows * leaf
    f32, bf16 = jnp.float32, jnp.bfloat16

    loads = [
        pltpu.make_async_copy(source, target, load_sem.at[position])
        for position, (source, target) in enumerate(
            [(right_hbm, right), (left_hbm, left), (near_hbm, near)]
        )
    ]
    for load in loads:
        load.start()

    barrier = pltpu.get_barrier_semaphore()

    def greet(step, carry):
        pl.semaphore_signal(
            barrier, inc=1, device_id={"rows": lax.rem(me + step, n)}, device_id_type=MESH
        )
        return carry

    lax.fori_loop(1, n, greet, 0, unroll=n <= 16)
    pl.semaphore_wait(barrier, n - 1)

    def send(phase, source, target):
        def one(step, carry):
            peer = lax.rem(me + step, n)
            pltpu.make_async_remote_copy(
                src_ref=source(peer),
                dst_ref=target.at[me],
                send_sem=send_sem.at[phase],
                recv_sem=recv_sem.at[phase],
                device_id={"rows": peer},
                device_id_type=MESH,
            ).start()
            return carry

        lax.fori_loop(1, n, one, 0, unroll=n <= 16)

    def arrived(phase, target):
        others = target.at[pl.ds(0, n - 1)]
        pltpu.make_async_copy(others, others, recv_sem.at[phase]).wait()

    def sent(phase, target):
        others = target.at[pl.ds(0, n - 1)]
        pltpu.make_async_copy(others, others, send_sem.at[phase]).wait()

    send(0, lambda peer: potential, whole_p)
    whole_p[me] = potential[...]

    def iota(shape, axis):
        return lax.broadcasted_iota(jnp.int32, shape, axis)

    eye = iota((blocks, blocks), 0) == iota((blocks, blocks), 1)
    col_place = jnp.sum(jnp.where(eye, col_local[...].astype(f32), 0.0), axis=1, keepdims=True)
    col_global = col_owner[...].astype(f32) * clusters + col_place
    pick = (iota((blocks, rows), 1).astype(f32) == col_global).astype(f32).astype(bf16)
    row_place = jnp.sum(jnp.where(eye, row_owner[...].astype(f32), 0.0), axis=0, keepdims=True)
    row_global = row_place * clusters + row_local[...].astype(f32)
    place = (iota((rows, blocks), 0).astype(f32) == row_global).astype(f32).astype(bf16)
    for start in range(0, masks.shape[1], leaf):
        lane = start + iota((blocks, leaf), 1)
        if start < near_count * leaf:
            owner = lane // leaf
        else:
            owner = near_count + (lane - near_count * leaf) // rank
        spread = (owner == iota((blocks, leaf), 0)).astype(f32).astype(bf16)
        masks[:, start : start + leaf] = jnp.dot(
            place, spread, preferred_element_type=f32
        ).astype(bf16)
    shape = (far_count, far_count)
    ranks = jnp.sum(
        jnp.where(iota(shape, 0) == iota(shape, 1), far_rank[...].astype(f32), 0.0),
        axis=1, keepdims=True,
    )
    for base in range(0, far_count, 16):
        lane = iota((16, 16 * rank), 1)
        inside = (lane // rank == iota((16, 16 * rank), 0)) & (
            (lane % rank).astype(f32) < ranks[base : base + 16]
        )
        rank_masks[base : base + 16] = inside.astype(f32)

    def wide(row):
        return jnp.broadcast_to(row, (16, row.shape[1])).astype(bf16)

    def spread_out(start, row):
        width = row.shape[1]
        mask = masks[:, start : start + width].reshape(rows // 16, 16, width)
        return (mask * wide(row)[None]).reshape(rows, width)

    def product(vector, field, first_time):
        picked = jnp.dot(pick, vector.astype(bf16), preferred_element_type=f32)
        if first_time:
            loads[0].wait()
        weights = []
        for base in range(0, far_count, 16):
            part = picked[near_count + base : near_count + base + 16].astype(bf16)
            levels = lax.dot_general(
                part, right[base : base + 16].reshape(16 * rank, leaf),
                (((1,), (1,)), ((), ())), preferred_element_type=f32,
            )
            weights.append(
                jnp.sum(levels * rank_masks[base : base + 16], axis=0, keepdims=True)
            )
        if first_time:
            loads[1].wait()
            loads[2].wait()
        result = jnp.zeros((rows, leaf), f32)
        for block in range(near_count):
            result += lax.dot_general(
                spread_out(block * leaf, picked[block : block + 1]), near[block],
                (((1,), (1,)), ((), ())), preferred_element_type=f32,
            )
        for base in range(0, far_count, 16):
            result += jnp.dot(
                spread_out(near_count * leaf + base * rank, weights[base // 16]),
                left[base : base + 16].reshape(16 * rank, leaf),
                preferred_element_type=f32,
            )
        field[...] = result.reshape(n, clusters, leaf)

    def reduce(phase, field, parts):
        send(phase, lambda peer: field.at[peer], parts)
        parts[me] = field[me]

    arrived(0, whole_p)
    pot = whole_p[...].reshape(rows, leaf)
    beta = jnp.sqrt(total(pot * pot) / panels + EPSILON)
    first = pot / beta
    product(first, field_one, True)
    reduce(1, field_one, parts_one)
    arrived(1, parts_one)
    mine[...] = jnp.sum(parts_one[...], axis=0)
    send(2, lambda peer: mine, whole_i)
    whole_i[me] = mine[...]
    first = whole_p[...].reshape(rows, leaf) / beta
    arrived(2, whole_i)
    image = whole_i[...].reshape(rows, leaf)
    h11 = total(image * first) / panels
    image = image - h11 * first
    h21 = jnp.sqrt(total(image * image) / panels + EPSILON)
    second = image / h21
    product(second, field_two, False)
    reduce(3, field_two, parts_two)
    g11 = total(first * first) / panels
    g12 = total(first * second) / panels
    g22 = total(second * second) / panels
    own_first = whole_p[me] / beta
    own_second = (whole_i[me] - h11 * own_first) / h21
    arrived(3, parts_two)
    own = jnp.sum(parts_two[...], axis=0)

    def fold(values):
        values = jnp.sum(values, axis=0, keepdims=True)
        return sum(values[:, at : at + 128] for at in range(0, leaf, 128))

    sums[me, 0:1] = fold(own * own_first)
    sums[me, 1:2] = fold(own * own_second)
    sums[me, 2:3] = fold(own * own)
    sums[me, 3:4] = jnp.zeros((1, 128), f32)
    send(4, lambda peer: sums.at[me], sums)
    arrived(4, sums)
    moments = jnp.sum(jnp.sum(sums[...], axis=0), axis=1, keepdims=True) / panels
    h12, h22, squared = moments[0:1], moments[1:2], moments[2:3]
    squared = (
        squared - 2.0 * (h12 * h12 + h22 * h22)
        + h12 * h12 * g11 + 2.0 * h12 * h22 * g12 + h22 * h22 * g22
    )
    h32 = jnp.sqrt(jnp.maximum(squared, 0.0) + EPSILON)
    krylov[0] = own_second
    krylov[1] = (own - h12 * own_first - h22 * own_second) / h32
    lane = iota(hessen.shape, 1)
    line = jnp.zeros(hessen.shape, f32)
    for position, value in enumerate([beta, h11, h21, h12, h22, h32]):
        line = jnp.where(lane == position, value, line)
    hessen[...] = line
    for phase, target in enumerate([whole_p, parts_one, whole_i, parts_two, sums]):
        sent(phase, target)


def on_device(
    potential, near_tiles, far_left, far_right, col_owner, col_local, row_owner, row_local, far_rank
):
    n = lax.axis_size("rows")
    clusters, leaf = potential.shape
    blocks = col_owner.shape[0]
    near_count = near_tiles.shape[0]
    far_count, rank = far_left.shape[:2]
    rows = n * clusters
    f32, bf16 = jnp.float32, jnp.bfloat16
    vmem = pl.BlockSpec(memory_space=pltpu.VMEM)
    anywhere = pl.BlockSpec(memory_space=pl.ANY)
    slabs = pltpu.VMEM((n, clusters, leaf), f32)
    krylov, hessen = pl.pallas_call(
        functools.partial(kernel, n),
        out_shape=(
            jax.ShapeDtypeStruct((2, clusters, leaf), f32),
            jax.ShapeDtypeStruct((1, 6), f32),
        ),
        in_specs=[vmem, anywhere, anywhere, anywhere] + [vmem] * 5,
        out_specs=(vmem, vmem),
        scratch_shapes=[
            pltpu.VMEM(near_tiles.shape, bf16),
            pltpu.VMEM(far_left.shape, bf16),
            pltpu.VMEM(far_right.shape, bf16),
            pltpu.VMEM((rows, near_count * leaf + far_count * rank), bf16),
            pltpu.VMEM((far_count, 16 * rank), f32),
            slabs, slabs, slabs, slabs, slabs, slabs,
            pltpu.VMEM((clusters, leaf), f32),
            pltpu.VMEM((n, 4, 128), f32),
            pltpu.SemaphoreType.DMA((3,)),
            pltpu.SemaphoreType.DMA((5,)),
            pltpu.SemaphoreType.DMA((5,)),
        ],
        compiler_params=pltpu.CompilerParams(
            collective_id=0, has_side_effects=True, vmem_limit_bytes=56 * 1024 * 1024
        ),
        name="arnoldi",
    )(
        potential, near_tiles, far_left, far_right,
        col_owner, col_local.reshape(1, blocks), row_owner, row_local.reshape(1, blocks),
        far_rank.reshape(1, far_count),
    )
    return (krylov, hessen)


def solution(mesh):
    placed = (
        P(("groups", "rows"), None),
        P(("groups", "rows"), None, None),
        P(("groups", "rows"), None, None),
        P(("groups", "rows"), None, None),
        P(("groups", "rows"), None),
        P(("groups", "rows")),
        P(("groups", "rows"), None),
        P(("groups", "rows")),
        P(("groups", "rows")),
    )
    return jax.shard_map(
        on_device,
        mesh=mesh,
        in_specs=placed,
        out_specs=(P(None, ("groups", "rows"), None), P("groups", None)),
        check_vma=False,
    )
```

time: 337 us -> 43.3 us (0.13)
  blocking collectives: 190 us -> 0 us
  waiting for transfers between devices: 108 us -> 0 us
  Pallas kernels: 0 us -> 37.3 us
  between operations: 16.9 us -> 0.64 us
  other arithmetic: 12.3 us -> 0 us
  matrix products: 6.16 us -> 0 us
    psum x5 -> x0, blocking collectives: 155 us -> none  [the longest x2 60.2 us: orthonormal(): squared = lax.psum(jnp.sum(remainder * remainder), 'rows') / panel_count]
    reduce_scatter x2 -> x0, waiting for transfers between devices: 108 us -> none  [product(): result = lax.psum_scatter(field, 'rows', scatter_dimension=0, tiled=True)]
    pallas_call x0 -> x1, Pallas kernels: none -> 37.3 us  [on_device(): pl.pallas_call(functools.partial(kernel, n), out_shape=(jax.ShapeDtypeStr...]
    all_gather x2 -> x0, blocking collectives: 34.6 us -> none  [product(): whole = lax.all_gather(rounded, 'rows', axis=0, tiled=True)]
    reduce_sum x5 -> x0, other arithmetic: 8.06 us -> none  [the longest x2 4 us: orthonormal(): squared = lax.psum(jnp.sum(remainder * remainder), 'rows') / panel_count]
    dot_general x8 -> x0, matrix products: 6.16 us -> none  [the longest x2 2.55 us: product(): jnp.einsum('krj,kj->kr', far_right, picked[near_count:], preferred_elemen...]
    unnamed x16 -> x4, local copies, waits for them, and re-layouts: 0.74 us -> 5.15 us
  transfers between devices with their start and end apart: 2 -> 0, of which waited for: 2 -> 0; matrix products, arithmetic and copies ran while one was open for 0% -> 0% of each run, Pallas kernels for 0% -> 0%
where the time goes in v1:
time: 43.3 us; the launch traced here: 43.1 us
  Pallas kernels  37.3 us (86%)
  local copies, waits for them, and re-layouts  5.15 us (12%)
  between operations  0.64 us (1%)
    pallas_call x1, Pallas kernels, on_device(): pl.pallas_call(functools.partial(kernel, n), out_shape=(jax.ShapeDtypeStr...  37.3 us
    unnamed x4, local copies, waits for them, and re-layouts  5.15 us

profile of v1, /device:TPU:0, one launch (start us, length us, event | category | flops | bytes accessed | tf_op | source)
XLA Modules:
  0.0 43.1 jit_solution(1540963243305055665)
XLA Ops:
  0.6 1.4 %copy.11.col_owner = s32[64,1]{1,0:T(8,128)} copy(s32[64,1]{0,1:T(1,128)} %param.13) | data formatting | bytes 512 | tf_op args[4]
  2.0 1.4 %copy.12.row_owner = s32[64,1]{1,0:T(8,128)} copy(s32[64,1]{0,1:T(1,128)} %param.15) | data formatting | bytes 512 | tf_op args[6]
  3.3 37.3 %arnoldi.1 = (f32[2,8,256]{2,1,0:T(8,128)}, f32[1,6]{1,0:T(1,128)}) custom-call(f32[8,256]{1,0:T(8,128)} %potential.1, bf16[16,256,256]{2,1,0:T(8,128)(2,1)} %near_hbm.1, bf16[48,64,256]{2,1,0:T(8,128)(2,1)} %left_hbm.1, bf16[48,64,256]{2,1,0:T(8,128)(2,1)} %right_hbm.1, s32[64,1]{1,0:T(8,128)} %copy.11.col_owner, s32[1,64]{1,0:T(1,128)} %bitcast.3, ...), custom_call_target="tpu_custom_call" | custom-call | tf_op jit(solution)/shard_map/arnoldi/pallas_call | solution.py:221
  40.7 1.3 %copy.15 = f32[2,8,256]{2,1,0:T(8,128)} copy(f32[2,8,256]{2,1,0:T(8,128)} %get-tuple-element.4) | data formatting | bytes 32768
  42.0 1.1 %copy.16 = f32[1,6]{1,0:T(1,128)} copy(f32[1,6]{1,0:T(1,128)} %get-tuple-element.5) | data formatting | bytes 48

commit v2 on v1

--- a/solution.py
+++ b/solution.py
@@ -18,12 +18,12 @@
 def kernel(
     n, potential, near_hbm, left_hbm, right_hbm, col_owner, col_local, row_owner, row_local, far_rank,
     krylov, hessen,
-    near, left, right, masks, rank_masks, field_one, field_two, whole_p, whole_i, parts_one, parts_two,
+    near, left, right, rank_masks, field_one, field_two, whole_p, whole_i, parts_one, parts_two,
     mine, sums, load_sem, send_sem, recv_sem,
 ):
     me = lax.axis_index("rows")
     clusters, leaf = potential.shape
-    blocks = col_owner.shape[0]
+    blocks = col_owner.shape[1]
     near_count, far_count, rank = near.shape[0], left.shape[0], left.shape[1]
     rows = n * clusters
     panels = rows * leaf
@@ -49,9 +49,21 @@
     lax.fori_loop(1, n, greet, 0, unroll=n <= 16)
     pl.semaphore_wait(barrier, n - 1)
 
+    group, groups = me // 4, n // 4
+    upper = group // (groups // 2)
+    turned = group + upper * (groups - 1 - 2 * group)
+
+    def peer_at(step):
+        place = groups - 1 - step // 4
+        place = place - (step // 4 + turned) // (groups - 1)
+        place = place + upper * (groups - 1 - 2 * place)
+        last = step // (n - 4)
+        place = place + last * (group - place)
+        return place * 4 + lax.rem(me + 1 + lax.rem(step, 4), 4)
+
     def send(phase, source, target):
         def one(step, carry):
-            peer = lax.rem(me + step, n)
+            peer = peer_at(step)
             pltpu.make_async_remote_copy(
                 src_ref=source(peer),
                 dst_ref=target.at[me],
@@ -62,7 +74,7 @@
             ).start()
             return carry
 
-        lax.fori_loop(1, n, one, 0, unroll=n <= 16)
+        lax.fori_loop(0, n - 1, one, 0, unroll=n <= 16)
 
     def arrived(phase, target):
         others = target.at[pl.ds(0, n - 1)]
@@ -79,22 +91,11 @@
         return lax.broadcasted_iota(jnp.int32, shape, axis)
 
     eye = iota((blocks, blocks), 0) == iota((blocks, blocks), 1)
-    col_place = jnp.sum(jnp.where(eye, col_local[...].astype(f32), 0.0), axis=1, keepdims=True)
-    col_global = col_owner[...].astype(f32) * clusters + col_place
+    col_row = (col_owner[...] * clusters + col_local[...]).astype(f32)
+    col_global = jnp.sum(jnp.where(eye, col_row, 0.0), axis=1, keepdims=True)
     pick = (iota((blocks, rows), 1).astype(f32) == col_global).astype(f32).astype(bf16)
-    row_place = jnp.sum(jnp.where(eye, row_owner[...].astype(f32), 0.0), axis=0, keepdims=True)
-    row_global = row_place * clusters + row_local[...].astype(f32)
+    row_global = (row_owner[...] * clusters + row_local[...]).astype(f32)
     place = (iota((rows, blocks), 0).astype(f32) == row_global).astype(f32).astype(bf16)
-    for start in range(0, masks.shape[1], leaf):
-        lane = start + iota((blocks, leaf), 1)
-        if start < near_count * leaf:
-            owner = lane // leaf
-        else:
-            owner = near_count + (lane - near_count * leaf) // rank
-        spread = (owner == iota((blocks, leaf), 0)).astype(f32).astype(bf16)
-        masks[:, start : start + leaf] = jnp.dot(
-            place, spread, preferred_element_type=f32
-        ).astype(bf16)
     shape = (far_count, far_count)
     ranks = jnp.sum(
         jnp.where(iota(shape, 0) == iota(shape, 1), far_rank[...].astype(f32), 0.0),
@@ -107,43 +108,47 @@
         )
         rank_masks[base : base + 16] = inside.astype(f32)
 
-    def wide(row):
-        return jnp.broadcast_to(row, (16, row.shape[1])).astype(bf16)
-
-    def spread_out(start, row):
-        width = row.shape[1]
-        mask = masks[:, start : start + width].reshape(rows // 16, 16, width)
-        return (mask * wide(row)[None]).reshape(rows, width)
+    side = (((1,), (1,)), ((), ()))
 
     def product(vector, field, first_time):
-        picked = jnp.dot(pick, vector.astype(bf16), preferred_element_type=f32)
+        picked = jnp.dot(pick, vector.astype(bf16), preferred_element_type=f32).astype(bf16)
         if first_time:
             loads[0].wait()
         weights = []
         for base in range(0, far_count, 16):
-            part = picked[near_count + base : near_count + base + 16].astype(bf16)
+            part = picked[near_count + base : near_count + base + 16]
             levels = lax.dot_general(
-                part, right[base : base + 16].reshape(16 * rank, leaf),
-                (((1,), (1,)), ((), ())), preferred_element_type=f32,
+                part, right[base : base + 16].reshape(16 * rank, leaf), side,
+                preferred_element_type=f32,
             )
-            weights.append(
-                jnp.sum(levels * rank_masks[base : base + 16], axis=0, keepdims=True)
-            )
+            weights.append((levels * rank_masks[base : base + 16]).astype(bf16))
+        if first_time:
+            loads[2].wait()
+        results = []
+        for base in range(0, near_count, 16):
+            part = picked[base : base + 16]
+            chosen = jnp.zeros((16, leaf), f32)
+            for block in range(16):
+                applied = lax.dot_general(
+                    part, near[base + block], side, preferred_element_type=f32
+                )
+                chosen = jnp.where(iota((16, leaf), 0) == block, applied, chosen)
+            results.append(chosen)
         if first_time:
             loads[1].wait()
-            loads[2].wait()
+        for base in range(0, far_count, 16):
+            results.append(
+                jnp.dot(
+                    weights[base // 16], left[base : base + 16].reshape(16 * rank, leaf),
+                    preferred_element_type=f32,
+                )
+            )
+        rest = jnp.concatenate(results, axis=0)
         result = jnp.zeros((rows, leaf), f32)
-        for block in range(near_count):
-            result += lax.dot_general(
-                spread_out(block * leaf, picked[block : block + 1]), near[block],
-                (((1,), (1,)), ((), ())), preferred_element_type=f32,
-            )
-        for base in range(0, far_count, 16):
-            result += jnp.dot(
-                spread_out(near_count * leaf + base * rank, weights[base // 16]),
-                left[base : base + 16].reshape(16 * rank, leaf),
-                preferred_element_type=f32,
-            )
+        for _ in range(3):
+            term = rest.astype(bf16)
+            rest = rest - term.astype(f32)
+            result += jnp.dot(place, term, preferred_element_type=f32)
         field[...] = result.reshape(n, clusters, leaf)
 
     def reduce(phase, field, parts):
@@ -205,6 +210,11 @@
         sent(phase, target)
 
 
+def hand_over(krylov_in, hessen_in, krylov, hessen):
+    krylov[...] = krylov_in[...]
+    hessen[...] = hessen_in[...]
+
+
 def on_device(
     potential, near_tiles, far_left, far_right, col_owner, col_local, row_owner, row_local, far_rank
 ):
@@ -230,7 +240,6 @@
             pltpu.VMEM(near_tiles.shape, bf16),
             pltpu.VMEM(far_left.shape, bf16),
             pltpu.VMEM(far_right.shape, bf16),
-            pltpu.VMEM((rows, near_count * leaf + far_count * rank), bf16),
             pltpu.VMEM((far_count, 16 * rank), f32),
             slabs, slabs, slabs, slabs, slabs, slabs,
             pltpu.VMEM((clusters, leaf), f32),
@@ -245,10 +254,20 @@
         name="arnoldi",
     )(
         potential, near_tiles, far_left, far_right,
-        col_owner, col_local.reshape(1, blocks), row_owner, row_local.reshape(1, blocks),
+        col_owner.reshape(1, blocks), col_local.reshape(1, blocks),
+        row_owner.reshape(1, blocks), row_local.reshape(1, blocks),
         far_rank.reshape(1, far_count),
     )
-    return (krylov, hessen)
+    return pl.pallas_call(
+        hand_over,
+        out_shape=(
+            jax.ShapeDtypeStruct((2, clusters, leaf), f32),
+            jax.ShapeDtypeStruct((1, 6), f32),
+        ),
+        in_specs=[vmem, vmem],
+        out_specs=(vmem, vmem),
+        name="hand_over",
+    )(krylov, hessen)
 
 
 def solution(mesh):

time: 43.3 us -> 37 us (0.85)
  local copies, waits for them, and re-layouts: 5.15 us -> 0 us
  Pallas kernels: 37.3 us -> 36.1 us
    unnamed x4 -> x0, local copies, waits for them, and re-layouts: 5.15 us -> none
    pallas_call x1, Pallas kernels: 37.3 us -> 34.8 us  [on_device(): pl.pallas_call(functools.partial(kernel, n), out_shape=(jax.ShapeDtypeStr...]
    pallas_call x0 -> x1, Pallas kernels: none -> 1.33 us  [on_device(): pl.pallas_call(hand_over, out_shape=(jax.ShapeDtypeStruct((2, clusters, l...]
where the time goes in v2:
time: 37 us; the launch traced here: 36.7 us
  Pallas kernels  36.1 us (98%)
  between operations  0.64 us (2%)
    pallas_call x1, Pallas kernels, on_device(): pl.pallas_call(functools.partial(kernel, n), out_shape=(jax.ShapeDtypeStr...  34.8 us
    pallas_call x1, Pallas kernels, on_device(): pl.pallas_call(hand_over, out_shape=(jax.ShapeDtypeStruct((2, clusters, l...  1.33 us

profile of v2, /device:TPU:0, one launch (start us, length us, event | category | flops | bytes accessed | tf_op | source)
XLA Modules:
  0.0 36.7 jit_solution(14220950189332247067)
XLA Ops:
  0.6 34.8 %arnoldi.1 = (f32[2,8,256]{2,1,0:T(8,128)}, f32[1,6]{1,0:T(1,128)}) custom-call(f32[8,256]{1,0:T(8,128)} %potential.1, bf16[16,256,256]{2,1,0:T(8,128)(2,1)} %near_hbm.1, bf16[48,64,256]{2,1,0:T(8,128)(2,1)} %left_hbm.1, bf16[48,64,256]{2,1,0:T(8,128)(2,1)} %right_hbm.1, s32[1,64]{1,0:T(1,128)} %bitcast.5, s32[1,64]{1,0:T(1,128)} %bitcast.6, ...), custom_call_target="tpu_custom_call" | custom-call | tf_op jit(solution)/shard_map/arnoldi/pallas_call | solution.py:231
  35.4 1.3 %hand_over.1 = (f32[2,8,256]{2,1,0:T(8,128)}, f32[1,6]{1,0:T(1,128)}) custom-call(f32[2,8,256]{2,1,0:T(8,128)} %get-tuple-element.4.krylov_in, f32[1,6]{1,0:T(1,128)} %get-tuple-element.5.hessen_in), custom_call_target="tpu_custom_call" | custom-call | tf_op jit(solution)/shard_map/hand_over/pallas_call | solution.py:261

commit v3 on v2

--- a/solution.py
+++ b/solution.py
@@ -16,10 +16,12 @@
 
 
 def kernel(
-    n, potential, near_hbm, left_hbm, right_hbm, col_owner, col_local, row_owner, row_local, far_rank,
+    n, potential_in, near_hbm, left_hbm, right_hbm, col_owner_in, col_local_in, row_owner_in,
+    row_local_in, far_rank_in,
     krylov, hessen,
+    potential, col_owner, col_local, row_owner, row_local, far_rank,
     near, left, right, rank_masks, field_one, field_two, whole_p, whole_i, parts_one, parts_two,
-    mine, sums, load_sem, send_sem, recv_sem,
+    sums, load_sem, send_sem, recv_sem,
 ):
     me = lax.axis_index("rows")
     clusters, leaf = potential.shape
@@ -29,41 +31,42 @@
     panels = rows * leaf
     f32, bf16 = jnp.float32, jnp.bfloat16
 
+    group, groups = lax.div(me, 4), n // 4
+    upper = lax.div(group, groups // 2)
+    turned = group + upper * (groups - 1 - 2 * group)
+
+    def peer_at(step):
+        place = groups - 1 - step // 4
+        place = place - lax.div(step // 4 + turned, groups - 1)
+        place = place + upper * (groups - 1 - 2 * place)
+        last = step // (n - 4)
+        place = place + last * (group - place)
+        return place * 4 + lax.rem(me + 1 + step % 4, 4)
+
+    peers = [peer_at(step) for step in range(n - 1)]
+
+    barrier = pltpu.get_barrier_semaphore()
+    for peer in peers:
+        pl.semaphore_signal(barrier, inc=1, device_id={"rows": peer}, device_id_type=MESH)
+
     loads = [
         pltpu.make_async_copy(source, target, load_sem.at[position])
         for position, (source, target) in enumerate(
-            [(right_hbm, right), (left_hbm, left), (near_hbm, near)]
+            [
+                (right_hbm, right), (left_hbm, left), (near_hbm, near), (potential_in, potential),
+                (col_owner_in, col_owner), (col_local_in, col_local), (row_owner_in, row_owner),
+                (row_local_in, row_local), (far_rank_in, far_rank),
+            ]
         )
     ]
-    for load in loads:
+    for load in loads[3:] + loads[:3]:
         load.start()
-
-    barrier = pltpu.get_barrier_semaphore()
-
-    def greet(step, carry):
-        pl.semaphore_signal(
-            barrier, inc=1, device_id={"rows": lax.rem(me + step, n)}, device_id_type=MESH
-        )
-        return carry
-
-    lax.fori_loop(1, n, greet, 0, unroll=n <= 16)
+    for load in loads[3:]:
+        load.wait()
     pl.semaphore_wait(barrier, n - 1)
 
-    group, groups = me // 4, n // 4
-    upper = group // (groups // 2)
-    turned = group + upper * (groups - 1 - 2 * group)
-
-    def peer_at(step):
-        place = groups - 1 - step // 4
-        place = place - (step // 4 + turned) // (groups - 1)
-        place = place + upper * (groups - 1 - 2 * place)
-        last = step // (n - 4)
-        place = place + last * (group - place)
-        return place * 4 + lax.rem(me + 1 + lax.rem(step, 4), 4)
-
     def send(phase, source, target):
-        def one(step, carry):
-            peer = peer_at(step)
+        for peer in peers:
             pltpu.make_async_remote_copy(
                 src_ref=source(peer),
                 dst_ref=target.at[me],
@@ -72,9 +75,6 @@
                 device_id={"rows": peer},
                 device_id_type=MESH,
             ).start()
-            return carry
-
-        lax.fori_loop(0, n - 1, one, 0, unroll=n <= 16)
 
     def arrived(phase, target):
         others = target.at[pl.ds(0, n - 1)]
@@ -95,7 +95,10 @@
     col_global = jnp.sum(jnp.where(eye, col_row, 0.0), axis=1, keepdims=True)
     pick = (iota((blocks, rows), 1).astype(f32) == col_global).astype(f32).astype(bf16)
     row_global = (row_owner[...] * clusters + row_local[...]).astype(f32)
-    place = (iota((rows, blocks), 0).astype(f32) == row_global).astype(f32).astype(bf16)
+    row_column = jnp.sum(jnp.where(eye, row_global, 0.0), axis=1, keepdims=True)
+    thrice = lax.rem(iota((blocks, 3 * blocks), 1), blocks) == iota((blocks, 3 * blocks), 0)
+    row_thrice = jnp.sum(jnp.where(thrice, row_column, 0.0), axis=0, keepdims=True)
+    place = (iota((rows, 3 * blocks), 0).astype(f32) == row_thrice).astype(f32).astype(bf16)
     shape = (far_count, far_count)
     ranks = jnp.sum(
         jnp.where(iota(shape, 0) == iota(shape, 1), far_rank[...].astype(f32), 0.0),
@@ -144,11 +147,11 @@
                 )
             )
         rest = jnp.concatenate(results, axis=0)
-        result = jnp.zeros((rows, leaf), f32)
+        terms = []
         for _ in range(3):
-            term = rest.astype(bf16)
-            rest = rest - term.astype(f32)
-            result += jnp.dot(place, term, preferred_element_type=f32)
+            terms.append(rest.astype(bf16))
+            rest = rest - terms[-1].astype(f32)
+        result = jnp.dot(place, jnp.concatenate(terms, axis=0), preferred_element_type=f32)
         field[...] = result.reshape(n, clusters, leaf)
 
     def reduce(phase, field, parts):
@@ -162,12 +165,16 @@
     product(first, field_one, True)
     reduce(1, field_one, parts_one)
     arrived(1, parts_one)
-    mine[...] = jnp.sum(parts_one[...], axis=0)
-    send(2, lambda peer: mine, whole_i)
-    whole_i[me] = mine[...]
+    mine = jnp.sum(parts_one[...], axis=0)
+    middle = leaf // 2
+    whole_i[me] = jnp.concatenate([mine[:, :middle], mine[:, middle:]], axis=0).astype(bf16)
+    send(2, lambda peer: whole_i.at[me], whole_i)
     first = whole_p[...].reshape(rows, leaf) / beta
     arrived(2, whole_i)
-    image = whole_i[...].reshape(rows, leaf)
+    image = whole_i[...].astype(f32)
+    image = jnp.concatenate(
+        [image[:, :clusters].reshape(rows, middle), image[:, clusters:].reshape(rows, middle)], axis=1
+    )
     h11 = total(image * first) / panels
     image = image - h11 * first
     h21 = jnp.sqrt(total(image * image) / panels + EPSILON)
@@ -178,7 +185,7 @@
     g12 = total(first * second) / panels
     g22 = total(second * second) / panels
     own_first = whole_p[me] / beta
-    own_second = (whole_i[me] - h11 * own_first) / h21
+    own_second = (mine - h11 * own_first) / h21
     arrived(3, parts_two)
     own = jnp.sum(parts_two[...], axis=0)
 
@@ -208,11 +215,6 @@
     hessen[...] = line
     for phase, target in enumerate([whole_p, parts_one, whole_i, parts_two, sums]):
         sent(phase, target)
-
-
-def hand_over(krylov_in, hessen_in, krylov, hessen):
-    krylov[...] = krylov_in[...]
-    hessen[...] = hessen_in[...]
 
 
 def on_device(
@@ -230,21 +232,25 @@
     slabs = pltpu.VMEM((n, clusters, leaf), f32)
     krylov, hessen = pl.pallas_call(
         functools.partial(kernel, n),
-        out_shape=(
-            jax.ShapeDtypeStruct((2, clusters, leaf), f32),
-            jax.ShapeDtypeStruct((1, 6), f32),
-        ),
-        in_specs=[vmem, anywhere, anywhere, anywhere] + [vmem] * 5,
+        out_shape=(pltpu.VMEM((2, clusters, leaf), f32), pltpu.VMEM((1, 6), f32)),
+        in_specs=[anywhere] * 9,
         out_specs=(vmem, vmem),
         scratch_shapes=[
+            pltpu.VMEM((clusters, leaf), f32),
+            pltpu.VMEM((1, blocks), jnp.int32),
+            pltpu.VMEM((1, blocks), jnp.int32),
+            pltpu.VMEM((1, blocks), jnp.int32),
+            pltpu.VMEM((1, blocks), jnp.int32),
+            pltpu.VMEM((1, far_count), jnp.int32),
             pltpu.VMEM(near_tiles.shape, bf16),
             pltpu.VMEM(far_left.shape, bf16),
             pltpu.VMEM(far_right.shape, bf16),
             pltpu.VMEM((far_count, 16 * rank), f32),
-            slabs, slabs, slabs, slabs, slabs, slabs,
-            pltpu.VMEM((clusters, leaf), f32),
+            slabs, slabs, slabs,
+            pltpu.VMEM((n, 2 * clusters, leaf // 2), bf16),
+            slabs, slabs,
             pltpu.VMEM((n, 4, 128), f32),
-            pltpu.SemaphoreType.DMA((3,)),
+            pltpu.SemaphoreType.DMA((9,)),
             pltpu.SemaphoreType.DMA((5,)),
             pltpu.SemaphoreType.DMA((5,)),
         ],
@@ -258,16 +264,7 @@
         row_owner.reshape(1, blocks), row_local.reshape(1, blocks),
         far_rank.reshape(1, far_count),
     )
-    return pl.pallas_call(
-        hand_over,
-        out_shape=(
-            jax.ShapeDtypeStruct((2, clusters, leaf), f32),
-            jax.ShapeDtypeStruct((1, 6), f32),
-        ),
-        in_specs=[vmem, vmem],
-        out_specs=(vmem, vmem),
-        name="hand_over",
-    )(krylov, hessen)
+    return (krylov, hessen)
 
 
 def solution(mesh):

time: 37 us -> 34 us (0.919)
  Pallas kernels: 36.1 us -> 32 us
  local copies, waits for them, and re-layouts: 0 us -> 1.12 us
    pallas_call x2 -> x1, Pallas kernels: 36.1 us -> 32 us  [on_device(): pl.pallas_call(functools.partial(kernel, n), out_shape=(pltpu.VMEM((2, cl...]
    unnamed x0 -> x2, local copies, waits for them, and re-layouts: none -> 1.12 us
where the time goes in v3:
time: 34 us; the launch traced here: 33.8 us
  Pallas kernels  32 us (94%)
  local copies, waits for them, and re-layouts  1.12 us (3%)
  between operations  0.64 us (2%)
    pallas_call x1, Pallas kernels, on_device(): pl.pallas_call(functools.partial(kernel, n), out_shape=(pltpu.VMEM((2, cl...  32 us
    unnamed x2, local copies, waits for them, and re-layouts  1.12 us

profile of v3, /device:TPU:0, one launch (start us, length us, event | category | flops | bytes accessed | tf_op | source)
XLA Modules:
  0.0 33.8 jit_solution(15951827717758880694)
XLA Ops:
  0.6 32.0 %arnoldi.1 = (f32[2,8,256]{2,1,0:T(8,128)S(1)}, f32[1,6]{1,0:T(1,128)S(1)}) custom-call(f32[8,256]{1,0:T(8,128)} %potential_in.1, bf16[16,256,256]{2,1,0:T(8,128)(2,1)} %near_hbm.1, bf16[48,64,256]{2,1,0:T(8,128)(2,1)} %left_hbm.1, bf16[48,64,256]{2,1,0:T(8,128)(2,1)} %right_hbm.1, s32[1,64]{1,0:T(1,128)} %bitcast.5, s32[1,64]{1,0:T(1,128)} %bitcast.6, ...), custom_call_target="tpu_custom_call" | custom-call | tf_op jit(solution)/shard_map/arnoldi/pallas_call | solution.py:233
  32.7 0.6 %copy.13 = f32[2,8,256]{2,1,0:T(8,128)} copy(f32[2,8,256]{2,1,0:T(8,128)S(1)} %get-tuple-element.2) | data formatting | bytes 32768
  33.3 0.5 %copy.14 = f32[1,6]{1,0:T(1,128)} copy(f32[1,6]{1,0:T(1,128)S(1)} %get-tuple-element.3) | data formatting | bytes 48

commit v4 on v3

--- a/solution.py
+++ b/solution.py
@@ -20,7 +20,7 @@
     row_local_in, far_rank_in,
     krylov, hessen,
     potential, col_owner, col_local, row_owner, row_local, far_rank,
-    near, left, right, rank_masks, field_one, field_two, whole_p, whole_i, parts_one, parts_two,
+    near, left, right, turned_right, rank_masks, field_one, field_two, whole_p, whole_i, parts_one, parts_two,
     sums, load_sem, send_sem, recv_sem,
 ):
     me = lax.axis_index("rows")
@@ -115,26 +115,23 @@
 
     def product(vector, field, first_time):
         picked = jnp.dot(pick, vector.astype(bf16), preferred_element_type=f32).astype(bf16)
-        if first_time:
-            loads[0].wait()
         weights = []
         for base in range(0, far_count, 16):
             part = picked[near_count + base : near_count + base + 16]
-            levels = lax.dot_general(
-                part, right[base : base + 16].reshape(16 * rank, leaf), side,
-                preferred_element_type=f32,
+            levels = jnp.concatenate(
+                [
+                    jnp.dot(part, turned_right[base // 4 + at], preferred_element_type=f32)
+                    for at in range(4)
+                ],
+                axis=1,
             )
             weights.append((levels * rank_masks[base : base + 16]).astype(bf16))
-        if first_time:
-            loads[2].wait()
         results = []
         for base in range(0, near_count, 16):
             part = picked[base : base + 16]
             chosen = jnp.zeros((16, leaf), f32)
             for block in range(16):
-                applied = lax.dot_general(
-                    part, near[base + block], side, preferred_element_type=f32
-                )
+                applied = jnp.dot(part, near[base + block], preferred_element_type=f32)
                 chosen = jnp.where(iota((16, leaf), 0) == block, applied, chosen)
             results.append(chosen)
         if first_time:
@@ -158,34 +155,43 @@
         send(phase, lambda peer: field.at[peer], parts)
         parts[me] = field[me]
 
+    loads[2].wait()
+    for block in range(near_count):
+        near[block] = near[block].T
+    loads[0].wait()
+    for base in range(0, far_count, 4):
+        turned_right[base // 4] = right[base : base + 4].reshape(4 * rank, leaf).T
     arrived(0, whole_p)
     pot = whole_p[...].reshape(rows, leaf)
     beta = jnp.sqrt(total(pot * pot) / panels + EPSILON)
-    first = pot / beta
-    product(first, field_one, True)
+    scale = 1.0 / beta
+    product(pot * scale, field_one, True)
     reduce(1, field_one, parts_one)
+    first = whole_p[...].reshape(rows, leaf) * scale
+    whole_p[...] = first.reshape(n, clusters, leaf)
+    g11 = total(first * first) / panels
     arrived(1, parts_one)
     mine = jnp.sum(parts_one[...], axis=0)
     middle = leaf // 2
     whole_i[me] = jnp.concatenate([mine[:, :middle], mine[:, middle:]], axis=0).astype(bf16)
     send(2, lambda peer: whole_i.at[me], whole_i)
-    first = whole_p[...].reshape(rows, leaf) / beta
+    first = whole_p[...].reshape(rows, leaf)
     arrived(2, whole_i)
     image = whole_i[...].astype(f32)
     image = jnp.concatenate(
         [image[:, :clusters].reshape(rows, middle), image[:, clusters:].reshape(rows, middle)], axis=1
     )
     h11 = total(image * first) / panels
-    image = image - h11 * first
-    h21 = jnp.sqrt(total(image * image) / panels + EPSILON)
-    second = image / h21
+    squared = total(image * image) / panels + h11 * h11 * (g11 - 2.0)
+    h21 = jnp.sqrt(jnp.maximum(squared, 0.0) + EPSILON)
+    scale = 1.0 / h21
+    second = (image - h11 * first) * scale
     product(second, field_two, False)
     reduce(3, field_two, parts_two)
-    g11 = total(first * first) / panels
     g12 = total(first * second) / panels
     g22 = total(second * second) / panels
-    own_first = whole_p[me] / beta
-    own_second = (mine - h11 * own_first) / h21
+    own_first = whole_p[me]
+    own_second = (mine - h11 * own_first) * scale
     arrived(3, parts_two)
     own = jnp.sum(parts_two[...], axis=0)
 
@@ -245,6 +251,7 @@
             pltpu.VMEM(near_tiles.shape, bf16),
             pltpu.VMEM(far_left.shape, bf16),
             pltpu.VMEM(far_right.shape, bf16),
+            pltpu.VMEM((far_count // 4, leaf, 4 * rank), bf16),
             pltpu.VMEM((far_count, 16 * rank), f32),
             slabs, slabs, slabs,
             pltpu.VMEM((n, 2 * clusters, leaf // 2), bf16),

time: 34 us -> 32.8 us (0.965)
  Pallas kernels: 32 us -> 30.9 us
    pallas_call x1, Pallas kernels: 32 us -> 30.9 us  [on_device(): pl.pallas_call(functools.partial(kernel, n), out_shape=(pltpu.VMEM((2, cl...]
where the time goes in v4:
time: 32.8 us; the launch traced here: 32.6 us
  Pallas kernels  30.9 us (94%)
  local copies, waits for them, and re-layouts  1.12 us (3%)
  between operations  0.64 us (2%)
    pallas_call x1, Pallas kernels, on_device(): pl.pallas_call(functools.partial(kernel, n), out_shape=(pltpu.VMEM((2, cl...  30.9 us
    unnamed x2, local copies, waits for them, and re-layouts  1.12 us

profile of v4, /device:TPU:0, one launch (start us, length us, event | category | flops | bytes accessed | tf_op | source)
XLA Modules:
  0.0 32.6 jit_solution(8746375285193964173)
XLA Ops:
  0.6 30.9 %arnoldi.1 = (f32[2,8,256]{2,1,0:T(8,128)S(1)}, f32[1,6]{1,0:T(1,128)S(1)}) custom-call(f32[8,256]{1,0:T(8,128)} %potential_in.1, bf16[16,256,256]{2,1,0:T(8,128)(2,1)} %near_hbm.1, bf16[48,64,256]{2,1,0:T(8,128)(2,1)} %left_hbm.1, bf16[48,64,256]{2,1,0:T(8,128)(2,1)} %right_hbm.1, s32[1,64]{1,0:T(1,128)} %bitcast.5, s32[1,64]{1,0:T(1,128)} %bitcast.6, ...), custom_call_target="tpu_custom_call" | custom-call | tf_op jit(solution)/shard_map/arnoldi/pallas_call | solution.py:239
  31.5 0.6 %copy.13 = f32[2,8,256]{2,1,0:T(8,128)} copy(f32[2,8,256]{2,1,0:T(8,128)S(1)} %get-tuple-element.2) | data formatting | bytes 32768
  32.1 0.5 %copy.14 = f32[1,6]{1,0:T(1,128)} copy(f32[1,6]{1,0:T(1,128)S(1)} %get-tuple-element.3) | data formatting | bytes 48

commit v5 on v4

--- a/solution.py
+++ b/solution.py
@@ -59,7 +59,7 @@
             ]
         )
     ]
-    for load in loads[3:] + loads[:3]:
+    for load in loads[3:] + [loads[0], loads[2], loads[1]]:
         load.start()
     for load in loads[3:]:
         load.wait()
@@ -155,12 +155,12 @@
         send(phase, lambda peer: field.at[peer], parts)
         parts[me] = field[me]
 
+    loads[0].wait()
+    for base in range(0, far_count, 4):
+        turned_right[base // 4] = right[base : base + 4].reshape(4 * rank, leaf).T
     loads[2].wait()
     for block in range(near_count):
         near[block] = near[block].T
-    loads[0].wait()
-    for base in range(0, far_count, 4):
-        turned_right[base // 4] = right[base : base + 4].reshape(4 * rank, leaf).T
     arrived(0, whole_p)
     pot = whole_p[...].reshape(rows, leaf)
     beta = jnp.sqrt(total(pot * pot) / panels + EPSILON)

time: 32.8 us -> 32.8 us (level)
  no operation moved by 1% of the time
where the time goes in v5:
time: 32.8 us; the launch traced here: 32.6 us
  Pallas kernels  30.9 us (94%)
  local copies, waits for them, and re-layouts  1.12 us (3%)
  between operations  0.64 us (2%)
    pallas_call x1, Pallas kernels, on_device(): pl.pallas_call(functools.partial(kernel, n), out_shape=(pltpu.VMEM((2, cl...  30.9 us
    unnamed x2, local copies, waits for them, and re-layouts  1.12 us

profile of v5, /device:TPU:0, one launch (start us, length us, event | category | flops | bytes accessed | tf_op | source)
XLA Modules:
  0.0 32.6 jit_solution(9495680840208488333)
XLA Ops:
  0.6 30.9 %arnoldi.1 = (f32[2,8,256]{2,1,0:T(8,128)S(1)}, f32[1,6]{1,0:T(1,128)S(1)}) custom-call(f32[8,256]{1,0:T(8,128)} %potential_in.1, bf16[16,256,256]{2,1,0:T(8,128)(2,1)} %near_hbm.1, bf16[48,64,256]{2,1,0:T(8,128)(2,1)} %left_hbm.1, bf16[48,64,256]{2,1,0:T(8,128)(2,1)} %right_hbm.1, s32[1,64]{1,0:T(1,128)} %bitcast.5, s32[1,64]{1,0:T(1,128)} %bitcast.6, ...), custom_call_target="tpu_custom_call" | custom-call | tf_op jit(solution)/shard_map/arnoldi/pallas_call | solution.py:239
  31.5 0.6 %copy.13 = f32[2,8,256]{2,1,0:T(8,128)} copy(f32[2,8,256]{2,1,0:T(8,128)S(1)} %get-tuple-element.2) | data formatting | bytes 32768
  32.1 0.5 %copy.14 = f32[1,6]{1,0:T(1,128)} copy(f32[1,6]{1,0:T(1,128)S(1)} %get-tuple-element.3) | data formatting | bytes 48
